TPU v7x, 128 devices: a whole 4x4x4 slice. The times are simulated.
128 devices in a mesh: row: 8 (over z, y_hi), col: 16 (over x, y_lo, core).
Axes of the slice: x: 4, y: 4 (y_hi: 2, y_lo: 2; y = y_hi * 2 + y_lo), z: 4, core: 2. Of those that a mesh axis runs over, the one named last changes fastest.
Arguments:
- val_wave: bfloat16 [8, 64, 64, 128], replicated, may hold values from -6 to 6
- cond_wave: bfloat16 [128, 64, 64, 128], P(('row', 'col')), may hold values from -6 to 6
- val_energy: float32 [8], replicated, may hold values from -12 to -0.5
- cond_energy: float32 [128], replicated, may hold values from 0.5 to 20
- band_owner: int32 [128], P(('row', 'col')), may hold values from 0 to 127, each once
- grid_map: int32 [30720], replicated, may hold values from 0 to 262143, as said below
Outputs:
- chi: float32 [2, 2048, 30720], P(None, 'row', 'col')
Inputs may be any that keep to these rules, and one draw needn't show every extreme that they name: `band_owner`: every one of the 128 band numbers stands in exactly one slot. `grid_map`: 30720 distinct flat grid points: those of the shortest wave vectors, with indices above 32 read as negative frequencies, ordered by length with ties in random order.
All inputs are finite; a program needn't handle non-finite values.
Results may differ from a plain program's by a relative error of at most 0.0041.
Values may be sent and summed in bfloat16 or wider, within the bound.
A program may use at most 576 MiB of HBM per device.

v0:
```python
import functools
import math

import jax
import jax.numpy as jnp
import ml_dtypes
import numpy as np
from jax import lax
from jax.experimental import pallas as pl
from jax.experimental.pallas import tpu as pltpu
from jax.sharding import PartitionSpec as P

GRID = 64
NG = 30720
SLAB = 2048
ROWS = 8
COLS = 16
G_COL = NG // COLS
G_ROW = SLAB // ROWS
MAGS = 20
CELLS = MAGS * MAGS
LANES = 128


def shells():
    points = np.arange(GRID)
    freq = np.where(points < GRID // 2, points, points - GRID)
    square = freq * freq
    length = (square[:, None, None] + square[None, :, None] + square[None, None, :]).ravel()
    length = np.sort(length, kind="stable")
    assert length[NG - 1] < MAGS * MAGS
    return length


def orbit_lists(width, count):
    length = shells()
    mags = np.arange(MAGS)
    a, b, c = np.meshgrid(mags, mags, mags, indexing="ij")
    a, b, c = a.ravel(), b.ravel(), c.ravel()
    square = a * a + b * b + c * c
    source = c * CELLS + (b // 4) * (4 * MAGS) + a * 4 + b % 4
    code = (a * GRID + b) * GRID + c
    lists = []
    for block in range(count):
        least, most = length[block * width], length[(block + 1) * width - 1]
        lists.append(np.nonzero((square >= least) & (square <= most))[0])
    rows = -(-max(len(picked) for picked in lists) // 16) * 16
    index = np.zeros((count, rows), np.int32)
    codes = np.full((count, 1, rows), -1, np.int32)
    for block, picked in enumerate(lists):
        index[block, : len(picked)] = source[picked]
        codes[block, 0, : len(picked)] = code[picked]
    return index, codes


def split_table(table):
    high = table.astype(ml_dtypes.bfloat16)
    low = (table - high.astype(np.float64)).astype(ml_dtypes.bfloat16)
    return np.concatenate([high, low], 0)


def dft_tables():
    point = np.arange(GRID)
    mag = np.arange(MAGS)
    angle = (mag[:, None] * point[None, :] % GRID) * (2.0 * math.pi / GRID)
    parts = np.stack([np.cos(angle), np.sin(angle)])
    table_b = np.zeros((2, MAGS // 4, 4, 4, 4, GRID))
    for a in range(4):
        table_b[:, :, a, :, a, :] = parts.reshape(2, MAGS // 4, 4, GRID)
    table_a = np.zeros((2, MAGS, 4, GRID, 4))
    for b in range(4):
        table_a[:, :, b, :, b] = parts
    table_c = np.zeros((MAGS, 2, 2, 2, 2, 2, GRID))
    for v in range(2):
        for sign in range(2):
            turn = 1.0 - 2.0 * sign
            table_c[:, v, 0, sign, 0, v] = parts[0]
            table_c[:, v, 0, sign, 1, v] = turn * parts[1]
            table_c[:, v, 1, sign, 1, v] = parts[0]
            table_c[:, v, 1, sign, 0, v] = -turn * parts[1]
    table_c = table_c * (1.0 / float(GRID) ** 1.5)
    return (
        split_table(table_b.reshape(8 * MAGS, 4 * GRID)),
        split_table(table_a.reshape(8 * MAGS, 4 * GRID)),
        split_table(table_c.reshape(8 * MAGS, 4 * GRID)),
    )


def dot_nn(left, right):
    return lax.dot_general(
        left, right, (((1,), (0,)), ((), ())), preferred_element_type=jnp.float32
    )


def dot_nt(left, right):
    return lax.dot_general(
        left, right, (((1,), (1,)), ((), ())), preferred_element_type=jnp.float32
    )


def halves(value):
    high = value.astype(jnp.bfloat16)
    return high, (value - high.astype(jnp.float32)).astype(jnp.bfloat16)


def three(dot, table, high, low):
    rows = table.shape[0] // 2
    both = dot(table, high)
    return both[:rows] + both[rows:] + dot(table[:rows], low)


def signs(both, rows):
    cos_re, cos_im = both[:rows, :LANES], both[:rows, LANES:]
    sin_re, sin_im = both[rows:, :LANES], both[rows:, LANES:]
    plus = jnp.concatenate([cos_re + sin_im, cos_im - sin_re], 1)
    minus = jnp.concatenate([cos_re - sin_im, cos_im + sin_re], 1)
    return plus, minus


def spectrum_kernel(
    owner, cond_energy, val_energy, index_p, index_w,
    val, cond, table_b, table_a, table_c,
    plain, weighted,
    zh, zl, uh, ul, sums, cells, picked,
):
    step = pl.program_id(0)
    block = 4 * GRID
    first = lax.broadcasted_iota(jnp.int32, (block, LANES), 1) < GRID
    tb = table_b[...]

    def along_b(t, carry):
        rows = pl.ds(t * 4, 4)
        slot = cond[0, rows].reshape(block, LANES).astype(jnp.float32)
        one = val[0, rows].reshape(block, LANES).astype(jnp.float32)
        two = val[1, rows].reshape(block, LANES).astype(jnp.float32)
        slot_t = pltpu.roll(slot, GRID, 1)
        one_t = pltpu.roll(one, GRID, 1)
        two_t = pltpu.roll(two, GRID, 1)
        slot_re = jnp.where(first, slot, slot_t)
        slot_im = jnp.where(first, slot_t, slot)
        val_re = jnp.where(first, one, two_t)
        val_im = jnp.where(first, one_t, two)
        dens_re = val_re * slot_re + val_im * slot_im
        dens_im = val_re * slot_im - val_im * slot_re
        high, low = halves(jnp.concatenate([dens_re, dens_im], 1))
        both = three(dot_nn, tb, high, low)
        out = pl.ds(pl.multiple_of(t * 16, 16), 16)
        for sign, value in enumerate(signs(both, 4 * MAGS)):
            high, low = halves(value)
            for group in range(MAGS // 4):
                zh[sign * 5 + group, out, :] = high[group * 16 : group * 16 + 16]
                zl[sign * 5 + group, out, :] = low[group * 16 : group * 16 + 16]
        return carry

    lax.fori_loop(0, GRID // 4, along_b, 0)
    ta = table_a[...]

    def along_a(group, carry):
        out = pl.ds(pl.multiple_of(group * 80, 16), 80)
        for sign_b in range(2):
            both = three(dot_nn, ta, zh[sign_b * 5 + group], zl[sign_b * 5 + group])
            for sign_a, value in enumerate(signs(both, 4 * MAGS)):
                high, low = halves(value)
                uh[sign_a * 2 + sign_b, out, :] = high
                ul[sign_a * 2 + sign_b, out, :] = low
        return carry

    lax.fori_loop(0, MAGS // 4, along_a, 0)
    tc = table_c[...]

    def along_c(pair, carry):
        value = three(dot_nt, tc, uh[pair], ul[pair])
        value = value.reshape(MAGS, 8, CELLS)
        sums[:, pl.ds(pl.multiple_of((pair * 4 + step) * 8, 8), 8), :CELLS] = value
        return carry

    lax.fori_loop(0, 4, along_c, 0)

    @pl.when(step == pl.num_programs(0) - 1)
    def _():
        def turn(mag, carry):
            value = jnp.transpose(sums[mag], (1, 0))
            cells[pl.ds(pl.multiple_of(mag * CELLS, 8), CELLS), :] = value[:CELLS]
            return carry

        lax.fori_loop(0, MAGS, turn, 0)
        lane = lax.broadcasted_iota(jnp.int32, (1, LANES), 1)
        band = (lane >> 3) % 4 * 2 + (lane >> 2) % 2
        gap = jnp.zeros((1, LANES), jnp.float32)
        energy = cond_energy[owner[0]]
        for v in range(8):
            gap = jnp.where(band == v, energy - val_energy[v], gap)
        weight = -2.0 / (math.sqrt(8 * LANES) * gap)
        rows = index_p.shape[1]

        def slab(block, carry):
            def row(i, inner):
                for k in range(16):
                    picked[pl.ds(i * 16 + k, 1), :] = cells[pl.ds(index_p[block, i * 16 + k], 1), :]
                return inner

            lax.fori_loop(0, rows // 16, row, 0)
            plain[block] = picked[...].astype(jnp.bfloat16)
            return carry

        lax.fori_loop(0, COLS, slab, 0)
        few = index_w.shape[1]

        def slab_w(block, carry):
            def row(i, inner):
                for k in range(16):
                    picked[pl.ds(i * 16 + k, 1), :] = cells[pl.ds(index_w[block, i * 16 + k], 1), :]
                return inner

            lax.fori_loop(0, few // 16, row, 0)
            weighted[block] = (picked[:few] * weight).astype(jnp.bfloat16)
            return carry

        lax.fori_loop(0, ROWS, slab_w, 0)


def spectra(val_wave, cond_wave, val_energy, cond_energy, band_owner):
    index_p, _ = orbit_lists(G_COL, COLS)
    index_w, _ = orbit_lists(G_ROW, ROWS)
    tables = dft_tables()
    smem = pl.BlockSpec(memory_space=pltpu.SMEM)
    whole = pl.BlockSpec((16 * MAGS, 4 * GRID), lambda i: (0, 0))
    return pl.pallas_call(
        spectrum_kernel,
        grid=(4,),
        in_specs=[smem] * 5
        + [
            pl.BlockSpec((2, GRID, GRID, LANES), lambda i: (i, 0, 0, 0)),
            pl.BlockSpec((1, GRID, GRID, LANES), lambda i: (0, 0, 0, 0)),
            whole, whole, whole,
        ],
        out_specs=[
            pl.BlockSpec((COLS, index_p.shape[1], LANES), lambda i: (0, 0, 0)),
            pl.BlockSpec((ROWS, index_w.shape[1], LANES), lambda i: (0, 0, 0)),
        ],
        out_shape=[
            jax.ShapeDtypeStruct((COLS, index_p.shape[1], LANES), jnp.bfloat16),
            jax.ShapeDtypeStruct((ROWS, index_w.shape[1], LANES), jnp.bfloat16),
        ],
        scratch_shapes=[
            pltpu.VMEM((10, 4 * GRID, 2 * LANES), jnp.bfloat16),
            pltpu.VMEM((10, 4 * GRID, 2 * LANES), jnp.bfloat16),
            pltpu.VMEM((4, CELLS, 2 * LANES), jnp.bfloat16),
            pltpu.VMEM((4, CELLS, 2 * LANES), jnp.bfloat16),
            pltpu.VMEM((MAGS, LANES, 512), jnp.float32),
            pltpu.VMEM((MAGS * CELLS, LANES), jnp.float32),
            pltpu.VMEM((index_p.shape[1], LANES), jnp.float32),
        ],
        compiler_params=pltpu.CompilerParams(vmem_limit_bytes=48 * 2**20),
        name="spectra",
    )(
        band_owner, cond_energy, val_energy, jnp.asarray(index_p), jnp.asarray(index_w),
        val_wave, cond_wave, *(jnp.asarray(table) for table in tables),
    )


def place_kernel(points, codes, slabs, fold, out):
    point = points[...]
    a, b, c = point >> 12, (point >> 6) & 63, point & 63
    half = GRID // 2
    code = (jnp.where(a > half, GRID - a, a) * GRID + jnp.where(b > half, GRID - b, b)) * GRID
    code = code + jnp.where(c > half, GRID - c, c)
    octant = (
        jnp.where(a > half, 4, 0) + jnp.where(b > half, 2, 0) + jnp.where(c > half, 1, 0)
    )
    hot = (code == codes[...]).astype(jnp.bfloat16)
    lane = lax.broadcasted_iota(jnp.int32, (1, LANES), 1)
    own = octant == (lane >> 5) * 2 + lane % 2
    total = None
    for source in range(slabs.shape[0]):
        row = dot_nn(hot, slabs[source])
        row = jnp.where(own, row, 0.0).astype(jnp.bfloat16)
        term = dot_nn(row, fold[source])
        total = term if total is None else total + term
    out[...] = total.astype(jnp.bfloat16)


def place(points, codes, slabs, tile):
    count, rows, _ = slabs.shape
    width = points.shape[0]
    fold = np.zeros((count, LANES, count * 16), ml_dtypes.bfloat16)
    lane = np.arange(LANES)
    for source in range(count):
        fold[source, lane, source * 16 + (lane >> 3) % 4 * 4 + (lane >> 1) % 4] = 1.0
    return pl.pallas_call(
        place_kernel,
        grid=(width // tile,),
        in_specs=[
            pl.BlockSpec((tile, 1), lambda i: (i, 0)),
            pl.BlockSpec((1, rows), lambda i: (0, 0)),
            pl.BlockSpec((count, rows, LANES), lambda i: (0, 0, 0)),
            pl.BlockSpec((count, LANES, count * 16), lambda i: (0, 0, 0)),
        ],
        out_specs=pl.BlockSpec((tile, count * 16), lambda i: (i, 0)),
        out_shape=jax.ShapeDtypeStruct((width, count * 16), jnp.bfloat16),
        compiler_params=pltpu.CompilerParams(vmem_limit_bytes=48 * 2**20),
        name="place",
    )(points.reshape(width, 1), codes, slabs, jnp.asarray(fold))


def product_kernel(left, panels, out):
    total = None
    depth = panels.shape[2]
    for source in range(panels.shape[0]):
        term = dot_nt(left[:, source * depth : (source + 1) * depth], panels[source])
        total = term if total is None else total + term
    out[...] = total.reshape(out.shape)


def product(left, panels, tile):
    count, width, depth = panels.shape
    return pl.pallas_call(
        product_kernel,
        grid=(width // tile,),
        in_specs=[
            pl.BlockSpec((2 * G_ROW, count * depth), lambda i: (0, 0)),
            pl.BlockSpec((count, tile, depth), lambda i: (0, i, 0)),
        ],
        out_specs=pl.BlockSpec((2, G_ROW, tile), lambda i: (0, 0, i)),
        out_shape=jax.ShapeDtypeStruct((2, G_ROW, width), jnp.float32),
        compiler_params=pltpu.CompilerParams(vmem_limit_bytes=48 * 2**20),
        name="product",
    )(left, panels)


def on_device(val_wave, cond_wave, val_energy, cond_energy, band_owner, grid_map):
    row = lax.axis_index("row")
    col = lax.axis_index("col")
    plain, weighted = spectra(val_wave, cond_wave, val_energy, cond_energy, band_owner)
    _, codes_p = orbit_lists(G_COL, COLS)
    _, codes_w = orbit_lists(G_ROW, ROWS)
    weighted = lax.all_to_all(weighted, "row", split_axis=0, concat_axis=0, tiled=True)
    plain = lax.all_to_all(plain, "col", split_axis=0, concat_axis=0, tiled=True)
    points_w = lax.dynamic_slice(grid_map, (row * G_ROW,), (G_ROW,))
    points_p = lax.dynamic_slice(grid_map, (col * G_COL,), (G_COL,))
    left = place(points_w, jnp.asarray(codes_w)[row], weighted, G_ROW)
    panel = place(points_p, jnp.asarray(codes_p)[col], plain, 384)
    left = lax.all_gather(left, "col", axis=0)
    panels = lax.all_gather(panel, "row", axis=0)
    left = left.reshape(COLS, G_ROW, ROWS, 8, 2).transpose(1, 2, 0, 3, 4)
    left_im = jnp.stack([left[..., 1], -left[..., 0]], -1)
    left = jnp.stack([left, left_im]).reshape(2 * G_ROW, ROWS * COLS * 16)
    return product(left, panels, 384)


def solution(mesh):
    in_specs = (P(), P(("row", "col"), None, None, None), P(), P(), P(("row", "col")), P())
    out_specs = P(None, "row", "col")
    return jax.shard_map(
        on_device, mesh=mesh, in_specs=in_specs, out_specs=out_specs, check_vma=False
    )
```

profile of v0, /device:TPU:1, one launch (start us, length us, event | category | flops | bytes accessed | tf_op | source)
XLA Modules:
  0.0 245.7 jit_solution(8911380831919642512)
XLA Ops:
  7.2 1.2 copy-done.1
  8.4 0.9 copy-done.3
  9.3 0.9 copy-done.4
  10.2 0.9 copy-done.5
  11.2 0.7 copy-done.6
  11.9 0.7 copy-done.7
  12.6 0.7 copy-done.8
  13.9 56.2 %spectra.1 = (bf16[16,320,128]{2,1,0:T(8,128)(2,1)}, bf16[8,64,128]{2,1,0:T(8,128)(2,1)}) custom-call(s32[1]{0:T(128)S(6)} %copy.24.owner, f32[128]{0:T(128)S(1)} %copy-done.8, f32[8]{0:T(128)S(1)} %copy-done.9, s32[16,320]{1,0:T(8,128)S(1)} %copy-done.6, s32[8,64]{1,0:T(8,128)S(1)} %copy-done.7, bf16[8,64,64,128]{3,2,1,0:T(8,128)(2,1)} %val.1, ...), custom_call_target="tpu_custom_call" | custom-call | tf_op jit(solution)/shard_map/spectra/pallas_call | solution.py:228
  70.1 8.5 %all-to-all-start = ((bf16[8,64,128]{2,1,0:T(8,128)(2,1)}), bf16[8,64,128]{2,1,0:T(8,128)(2,1)S(1)}, u32[]{:S(2)}, u32[]{:S(2)}) async-start(bf16[8,64,128]{2,1,0:T(8,128)(2,1)} %get-tuple-element.7), calls=%async_computation | async-start | bytes 262144 | tf_op jit(solution)/shard_map/all_to_all | solution.py:337
  78.6 0.8 dynamic_slice.12
  79.6 0.7 dynamic-slice_bitcast_fusion.1.codes
  80.2 5.4 %all-to-all-done.slabs = bf16[8,64,128]{2,1,0:T(8,128)(2,1)S(1)} async-done(((bf16[8,64,128]{2,1,0:T(8,128)(2,1)}), bf16[8,64,128]{2,1,0:T(8,128)(2,1)S(1)}, u32[]{:S(2)}, u32[]{:S(2)}) %all-to-all-start) | async-done | bytes 131104 | tf_op jit(solution)/shard_map/all_to_all | solution.py:337
  85.7 1.4 place.2
  87.0 6.6 %all-to-all-start.1 = ((bf16[16,320,128]{2,1,0:T(8,128)(2,1)}), bf16[16,320,128]{2,1,0:T(8,128)(2,1)S(1)}, u32[]{:S(2)}, u32[]{:S(2)}) async-start(bf16[16,320,128]{2,1,0:T(8,128)(2,1)} %get-tuple-element.8), calls=%async_computation.1 | async-start | bytes 2621440 | tf_op jit(solution)/shard_map/all_to_all | solution.py:338
  93.6 0.8 dynamic_slice.14
  94.7 0.7 dynamic-slice_bitcast_fusion.codes
  95.4 17.9 %all-to-all-done.1.slabs = bf16[16,320,128]{2,1,0:T(8,128)(2,1)S(1)} async-done(((bf16[16,320,128]{2,1,0:T(8,128)(2,1)}), bf16[16,320,128]{2,1,0:T(8,128)(2,1)S(1)}, u32[]{:S(2)}, u32[]{:S(2)}) %all-to-all-start.1) | async-done | bytes 1310752 | tf_op jit(solution)/shard_map/all_to_all | solution.py:338
  113.4 15.1 %place.3 = bf16[1920,256]{1,0:T(8,128)(2,1)} custom-call(s32[1920,1]{1,0:T(8,128)S(1)} %reshape.19.points, s32[1,320]{1,0:T(1,128)S(1)} %dynamic-slice_bitcast_fusion.codes, bf16[16,320,128]{2,1,0:T(8,128)(2,1)S(1)} %all-to-all-done.1.slabs, bf16[16,128,256]{2,1,0:T(8,128)(2,1)S(1)} %copy-done), custom_call_target="tpu_custom_call" | custom-call | tf_op jit(solution)/shard_map/place/pallas_call | solution.py:290
  128.6 1.5 copy.18
  130.7 2.2 copy.19
  132.9 1.8 copy.23
  134.7 3.0 %copy.21.left = bf16[512,2048]{1,0:T(8,128)(2,1)S(1)} copy(bf16[512,2048]{0,1:T(8,128)(2,1)} %bitcast.26) | data formatting | bytes 4194304 | tf_op jit(solution)/shard_map/reshape | solution.py:347
  137.7 91.6 %all-gather.7.cloned.1.call-done = bf16[15360,256]{1,0:T(8,128)(2,1)} async-done(((bf16[1920,256]{1,0:T(8,128)(2,1)}), bf16[15360,256]{1,0:T(8,128)(2,1)}) %all-gather.7.cloned.1.call-update) | async-done | bytes 7864336 | tf_op jit(solution)/shard_map/all_gather | solution.py:344
  229.3 9.5 %product.1 = f32[2,256,1920]{2,1,0:T(8,128)} custom-call(bf16[512,2048]{1,0:T(8,128)(2,1)S(1)} %copy.21.left, bf16[8,1920,256]{2,1,0:T(8,128)(2,1)} %bitcast.27), custom_call_target="tpu_custom_call" | custom-call | tf_op jit(solution)/shard_map/product/pallas_call | solution.py:317
  (24 shorter events, 1.9 us)
Async XLA Ops:
  7.2 1.2 copy-start.1
  8.4 0.9 copy-start.3
  9.3 0.9 copy-start.4
  10.2 0.9 copy-start.5
  11.2 0.7 copy-start.6
  11.9 0.7 copy-start.7
  12.6 0.7 copy-start.8
  13.2 0.7 copy-start.9
  13.9 71.8 %copy-start.2 = (bf16[8,128,128]{2,1,0:T(8,128)(2,1)S(1)}, bf16[8,128,128]{2,1,0:T(8,128)(2,1)}, u32[]{:S(2)}) copy-start(bf16[8,128,128]{2,1,0:T(8,128)(2,1)} %constant.45.clone.fold) | copy-start | bytes 786436
  70.1 15.6 %all-to-all-start = ((bf16[8,64,128]{2,1,0:T(8,128)(2,1)}), bf16[8,64,128]{2,1,0:T(8,128)(2,1)S(1)}, u32[]{:S(2)}, u32[]{:S(2)}) async-start(bf16[8,64,128]{2,1,0:T(8,128)(2,1)} %get-tuple-element.7), calls=%async_computation | async-start | bytes 262144 | tf_op jit(solution)/shard_map/all_to_all | solution.py:337
  78.6 50.0 %all-gather.5.cloned.1.call-start = ((), (), s32[]{:S(2)}) async-start(), calls=%async_computation.2 | async-start | bytes 1114112 | tf_op jit(solution)/shard_map/all_gather | solution.py:343
  80.2 33.2 %copy-start = (bf16[16,128,256]{2,1,0:T(8,128)(2,1)S(1)}, bf16[16,128,256]{2,1,0:T(8,128)(2,1)}, u32[]{:S(2)}) copy-start(bf16[16,128,256]{2,1,0:T(8,128)(2,1)} %constant.47.clone.fold) | copy-start | bytes 3145732
  87.0 26.3 %all-to-all-start.1 = ((bf16[16,320,128]{2,1,0:T(8,128)(2,1)}), bf16[16,320,128]{2,1,0:T(8,128)(2,1)S(1)}, u32[]{:S(2)}, u32[]{:S(2)}) async-start(bf16[16,320,128]{2,1,0:T(8,128)(2,1)} %get-tuple-element.8), calls=%async_computation.1 | async-start | bytes 2621440 | tf_op jit(solution)/shard_map/all_to_all | solution.py:338
  93.6 135.7 %all-gather.7.cloned.1.call-start = ((), (), s32[]{:S(2)}) async-start(), calls=%async_computation.3 | async-start | bytes 8847360 | tf_op jit(solution)/shard_map/all_gather | solution.py:344
Sparse Core Ops, SparseCore 0:
  87.2 39.3 all-gather.4
  128.8 100.4 all-gather.6
where the time goes:
time: 246 us
  waiting for transfers between devices  115 us (47%)
  Pallas kernels  82.2 us (33%)
  local copies, waits for them, and re-layouts  18.8 us (8%)
  starting transfers between devices  15.1 us (6%)
  between operations  14.2 us (6%)
    all_gather x1, waiting for transfers between devices, on_device(): panels = lax.all_gather(panel, 'row', axis=0)  91.6 us
    pallas_call x1, Pallas kernels, spectra(): pl.pallas_call(spectrum_kernel, grid=(4,), in_specs=[smem] * 5 + [pl.Bloc...  56.2 us
    all_to_all x1, waiting for transfers between devices, on_device(): lax.all_to_all(plain, 'col', split_axis=0, concat_axis=0, tiled=True)  17.9 us
    pallas_call x2, Pallas kernels, place(): pl.pallas_call(place_kernel, grid=(width // tile,), in_specs=[pl.BlockSpe...  16.5 us
    pallas_call x1, Pallas kernels, product(): pl.pallas_call(product_kernel, grid=(width // tile,), in_specs=[pl.BlockS...  9.51 us
    unnamed x22, local copies, waits for them, and re-layouts  8.79 us
    all_to_all x1, starting transfers between devices, on_device(): lax.all_to_all(weighted, 'row', split_axis=0, concat_axis=0, tiled=True)  8.5 us
    all_to_all x1, starting transfers between devices, on_device(): lax.all_to_all(plain, 'col', split_axis=0, concat_axis=0, tiled=True)  6.55 us
  transfers between devices with their start and end apart: 4, of which 3 were waited for; matrix products, arithmetic and copies ran while one was open for 5% of the time, Pallas kernels for 6%

commit v1 on v0

v1 whole, which is shorter than its diff:
```python
import functools
import math

import jax
import jax.numpy as jnp
import ml_dtypes
import numpy as np
from jax import lax
from jax.experimental import pallas as pl
from jax.experimental.pallas import tpu as pltpu
from jax.sharding import PartitionSpec as P

GRID = 64
NG = 30720
SLAB = 2048
ROWS = 8
COLS = 16
G_COL = NG // COLS
G_ROW = SLAB // ROWS
MAGS = 20
CELLS = MAGS * MAGS
LANES = 128


def shells():
    points = np.arange(GRID)
    freq = np.where(points < GRID // 2, points, points - GRID)
    square = freq * freq
    length = (square[:, None, None] + square[None, :, None] + square[None, None, :]).ravel()
    length = np.sort(length, kind="stable")
    assert length[NG - 1] < MAGS * MAGS
    return length


def orbit_lists(width, count):
    length = shells()
    mags = np.arange(MAGS)
    a, b, c = np.meshgrid(mags, mags, mags, indexing="ij")
    a, b, c = a.ravel(), b.ravel(), c.ravel()
    square = a * a + b * b + c * c
    source = c * CELLS + (b // 4) * (4 * MAGS) + a * 4 + b % 4
    code = (a * GRID + b) * GRID + c
    order = np.argsort(square, kind="stable")
    lists = []
    for block in range(count):
        least, most = length[block * width], length[(block + 1) * width - 1]
        lists.append(order[(square[order] >= least) & (square[order] <= most)])
    rows = -(-max(len(picked) for picked in lists) // 16) * 16
    index = np.zeros((count, rows), np.int32)
    codes = np.full((count, 1, rows), -1, np.int32)
    for block, picked in enumerate(lists):
        index[block, : len(picked)] = source[picked]
        codes[block, 0, : len(picked)] = code[picked]
    return index, codes, [square[picked] for picked in lists]


def windows(width, count, tile):
    length = shells()
    _, codes, squares = orbit_lists(width, count)
    starts, ends = [], []
    for at in range(0, width, tile):
        first, last = [], []
        for block, square in enumerate(squares):
            first.append(np.searchsorted(square, length[block * width + at], "left"))
            last.append(np.searchsorted(square, length[block * width + at + tile - 1], "right"))
        starts.append(int(min(first)) // 16 * 16)
        ends.append(int(max(last)))
    rows = max(-(-(end - start) // 16) * 16 for start, end in zip(starts, ends))
    return [min(start, codes.shape[2] - rows) for start in starts], rows


def split_table(table):
    high = table.astype(ml_dtypes.bfloat16)
    low = (table - high.astype(np.float64)).astype(ml_dtypes.bfloat16)
    return np.concatenate([high, low], 0)


def dft_tables():
    point = np.arange(GRID)
    mag = np.arange(MAGS)
    angle = (mag[:, None] * point[None, :] % GRID) * (2.0 * math.pi / GRID)
    parts = np.stack([np.cos(angle), np.sin(angle)])
    table_b = np.zeros((2, MAGS // 4, 4, 4, 4, GRID))
    for a in range(4):
        table_b[:, :, a, :, a, :] = parts.reshape(2, MAGS // 4, 4, GRID)
    table_a = np.zeros((2, MAGS, 4, GRID, 4))
    for b in range(4):
        table_a[:, :, b, :, b] = parts
    table_c = np.zeros((MAGS, 2, 2, 2, 2, 2, GRID))
    for v in range(2):
        for sign in range(2):
            turn = 1.0 - 2.0 * sign
            table_c[:, v, 0, sign, 0, v] = parts[0]
            table_c[:, v, 0, sign, 1, v] = turn * parts[1]
            table_c[:, v, 1, sign, 1, v] = parts[0]
            table_c[:, v, 1, sign, 0, v] = -turn * parts[1]
    table_c = table_c * (1.0 / float(GRID) ** 1.5)
    return (
        split_table(table_b.reshape(8 * MAGS, 4 * GRID)),
        split_table(table_a.reshape(8 * MAGS, 4 * GRID)),
        split_table(table_c.reshape(8 * MAGS, 4 * GRID)),
    )


def dot_nn(left, right):
    return lax.dot_general(
        left, right, (((1,), (0,)), ((), ())), preferred_element_type=jnp.float32
    )


def dot_nt(left, right):
    return lax.dot_general(
        left, right, (((1,), (1,)), ((), ())), preferred_element_type=jnp.float32
    )


def halves(value):
    high = value.astype(jnp.bfloat16)
    return high, (value - high.astype(jnp.float32)).astype(jnp.bfloat16)


def three(dot, table, high, low):
    rows = table.shape[0] // 2
    both = dot(table, high)
    return both[:rows] + both[rows:] + dot(table[:rows], low)


def signs(both, rows):
    cos_re, cos_im = both[:rows, :LANES], both[:rows, LANES:]
    sin_re, sin_im = both[rows:, :LANES], both[rows:, LANES:]
    plus = jnp.concatenate([cos_re + sin_im, cos_im - sin_re], 1)
    minus = jnp.concatenate([cos_re - sin_im, cos_im + sin_re], 1)
    return plus, minus


def spectrum_kernel(
    owner, cond_energy, val_energy, index_p, index_w,
    val, cond, table_b, table_a, table_c,
    plain, weighted,
    slots, zh, zl, uh, ul, sums, cells, picked,
):
    step = pl.program_id(0)
    block = 4 * GRID
    first = lax.broadcasted_iota(jnp.int32, (block, LANES), 1) < GRID
    tb = table_b[...]

    @pl.when(step == 0)
    def _():
        def widen(t, carry):
            slot = cond[0, pl.ds(t * 4, 4)].reshape(block, LANES).astype(jnp.float32)
            slot_t = pltpu.roll(slot, GRID, 1)
            slots[t, 0] = jnp.where(first, slot, slot_t)
            slots[t, 1] = jnp.where(first, slot_t, slot)
            return carry

        lax.fori_loop(0, GRID // 4, widen, 0)

    def along_b(t, carry):
        rows = pl.ds(t * 4, 4)
        one = val[0, rows].reshape(block, LANES).astype(jnp.float32)
        two = val[1, rows].reshape(block, LANES).astype(jnp.float32)
        one_t = pltpu.roll(one, GRID, 1)
        two_t = pltpu.roll(two, GRID, 1)
        slot_re, slot_im = slots[t, 0], slots[t, 1]
        val_re = jnp.where(first, one, two_t)
        val_im = jnp.where(first, one_t, two)
        dens_re = val_re * slot_re + val_im * slot_im
        dens_im = val_re * slot_im - val_im * slot_re
        high, low = halves(jnp.concatenate([dens_re, dens_im], 1))
        both = three(dot_nn, tb, high, low)
        out = pl.ds(pl.multiple_of(t * 16, 16), 16)
        for sign, value in enumerate(signs(both, 4 * MAGS)):
            high, low = halves(value)
            for group in range(MAGS // 4):
                zh[sign * 5 + group, out, :] = high[group * 16 : group * 16 + 16]
                zl[sign * 5 + group, out, :] = low[group * 16 : group * 16 + 16]
        return carry

    lax.fori_loop(0, GRID // 4, along_b, 0, unroll=2)
    ta = table_a[...]

    def along_a(group, carry):
        out = pl.ds(pl.multiple_of(group * 80, 16), 80)
        for sign_b in range(2):
            both = three(dot_nn, ta, zh[sign_b * 5 + group], zl[sign_b * 5 + group])
            for sign_a, value in enumerate(signs(both, 4 * MAGS)):
                high, low = halves(value)
                uh[sign_a * 2 + sign_b, out, :] = high
                ul[sign_a * 2 + sign_b, out, :] = low
        return carry

    lax.fori_loop(0, MAGS // 4, along_a, 0, unroll=True)
    tc = table_c[...]

    def along_c(pair, carry):
        value = three(dot_nt, tc, uh[pair], ul[pair])
        value = value.reshape(MAGS, 8, CELLS)
        sums[:, pl.ds(pl.multiple_of((pair * 4 + step) * 8, 8), 8), :CELLS] = value
        return carry

    lax.fori_loop(0, 4, along_c, 0, unroll=2)

    @pl.when(step == pl.num_programs(0) - 1)
    def _():
        def turn(mag, carry):
            value = jnp.transpose(sums[mag], (1, 0))
            cells[pl.ds(pl.multiple_of(mag * CELLS, 8), CELLS), :] = value[:CELLS]
            return carry

        lax.fori_loop(0, MAGS, turn, 0, unroll=2)
        lane = lax.broadcasted_iota(jnp.int32, (1, LANES), 1)
        band = (lane >> 3) % 4 * 2 + (lane >> 2) % 2
        gap = jnp.zeros((1, LANES), jnp.float32)
        energy = cond_energy[owner[0]]
        for v in range(8):
            gap = jnp.where(band == v, energy - val_energy[v], gap)
        weight = -2.0 / (math.sqrt(8 * LANES) * gap)
        def gather(index, count):
            def row(i, carry):
                for k in range(64):
                    picked[pl.ds(i * 64 + k, 1), :] = cells[pl.ds(index[i * 64 + k], 1), :]
                return carry

            lax.fori_loop(0, count // 64, row, 0)

        gather(index_p, plain.shape[0] * plain.shape[1])
        plain[...] = picked[...].astype(jnp.bfloat16).reshape(plain.shape)
        count = weighted.shape[0] * weighted.shape[1]
        gather(index_w, count)
        weighted[...] = (picked[:count] * weight).astype(jnp.bfloat16).reshape(weighted.shape)


def spectra(val_wave, cond_wave, val_energy, cond_energy, band_owner):
    index_p, _, _ = orbit_lists(G_COL, COLS)
    index_w, _, _ = orbit_lists(G_ROW, ROWS)
    tables = dft_tables()
    smem = pl.BlockSpec(memory_space=pltpu.SMEM)
    whole = pl.BlockSpec((16 * MAGS, 4 * GRID), lambda i: (0, 0))
    return pl.pallas_call(
        spectrum_kernel,
        grid=(4,),
        in_specs=[smem] * 5
        + [
            pl.BlockSpec((2, GRID, GRID, LANES), lambda i: (i, 0, 0, 0)),
            pl.BlockSpec((1, GRID, GRID, LANES), lambda i: (0, 0, 0, 0)),
            whole, whole, whole,
        ],
        out_specs=[
            pl.BlockSpec((COLS, index_p.shape[1], LANES), lambda i: (0, 0, 0)),
            pl.BlockSpec((ROWS, index_w.shape[1], LANES), lambda i: (0, 0, 0)),
        ],
        out_shape=[
            jax.ShapeDtypeStruct((COLS, index_p.shape[1], LANES), jnp.bfloat16),
            jax.ShapeDtypeStruct((ROWS, index_w.shape[1], LANES), jnp.bfloat16),
        ],
        scratch_shapes=[
            pltpu.VMEM((GRID // 4, 2, 4 * GRID, LANES), jnp.float32),
            pltpu.VMEM((10, 4 * GRID, 2 * LANES), jnp.bfloat16),
            pltpu.VMEM((10, 4 * GRID, 2 * LANES), jnp.bfloat16),
            pltpu.VMEM((4, CELLS, 2 * LANES), jnp.bfloat16),
            pltpu.VMEM((4, CELLS, 2 * LANES), jnp.bfloat16),
            pltpu.VMEM((MAGS, LANES, 512), jnp.float32),
            pltpu.VMEM((MAGS * CELLS, LANES), jnp.float32),
            pltpu.VMEM((index_p.size, LANES), jnp.float32),
        ],
        compiler_params=pltpu.CompilerParams(vmem_limit_bytes=48 * 2**20),
        name="spectra",
    )(
        band_owner, cond_energy, val_energy, jnp.asarray(index_p.ravel()), jnp.asarray(index_w.ravel()),
        val_wave, cond_wave, *(jnp.asarray(table) for table in tables),
    )


def placed(point, codes, slabs, fold):
    a, b, c = point >> 12, (point >> 6) & 63, point & 63
    half = GRID // 2
    code = (jnp.where(a > half, GRID - a, a) * GRID + jnp.where(b > half, GRID - b, b)) * GRID
    code = code + jnp.where(c > half, GRID - c, c)
    octant = (
        jnp.where(a > half, 4, 0) + jnp.where(b > half, 2, 0) + jnp.where(c > half, 1, 0)
    )
    hot = (code == codes).astype(jnp.bfloat16)
    lane = lax.broadcasted_iota(jnp.int32, (1, 2 * LANES), 1) % LANES
    own = octant == (lane >> 5) * 2 + lane % 2
    rows = []
    for pair in range(len(slabs) // 2):
        both = jnp.concatenate([slabs[2 * pair], slabs[2 * pair + 1]], 1)
        rows.append(jnp.where(own, dot_nn(hot, both), 0.0).astype(jnp.bfloat16))
    return dot_nn(jnp.concatenate(rows, 1), fold)


def fold_table(count):
    fold = np.zeros((count, LANES, count * 16), ml_dtypes.bfloat16)
    lane = np.arange(LANES)
    for source in range(count):
        fold[source, lane, source * 16 + (lane >> 3) % 4 * 4 + (lane >> 1) % 4] = 1.0
    return fold.reshape(count * LANES, count * 16)


def turn_table():
    table = np.zeros((2 * LANES, 2 * LANES), ml_dtypes.bfloat16)
    lane = np.arange(0, 2 * LANES, 2)
    table[lane + 1, lane] = 1.0
    table[lane, lane + 1] = -1.0
    return table


TILE = 384
TILES = G_COL // TILE
KINDS = 9


def exchange_kernel(
    points_p, points_w, codes_p, codes_w, plain, weighted, fold_p, fold_w, turn,
    out,
    slabs, slabs_w, lefts, left, panels, stage,
    col_send, col_recv, row_send, row_recv, left_send, left_recv, move_send, move_recv, own_sem, out_sem,
):
    row, col = lax.axis_index("row"), lax.axis_index("col")
    z, y_hi = row // 2, lax.rem(row, 2)
    x, y_lo, core = col // 4, lax.rem(col // 2, 2), lax.rem(col, 2)
    up, down, far = lax.rem(z + 1, 4), lax.rem(z + 3, 4), lax.rem(z + 2, 4)
    above, below = (up * 2 + y_hi, col), (down * 2 + y_hi, col)
    across_row = z * 2 + 1 - y_hi
    across = (across_row, col)
    slot = core * 8 + col // 2

    def push(src, dst, send, recv, device):
        return pltpu.make_async_remote_copy(
            src_ref=src, dst_ref=dst, send_sem=send, recv_sem=recv,
            device_id=device, device_id_type=pl.DeviceIdType.MESH,
        )

    barrier = pltpu.get_barrier_semaphore()
    for i in range(1, COLS):
        pl.semaphore_signal(
            barrier, inc=1, device_id=(row, lax.rem(col + i, COLS)),
            device_id_type=pl.DeviceIdType.MESH,
        )
    for i in range(1, ROWS):
        pl.semaphore_signal(
            barrier, inc=1, device_id=(lax.rem(row + i, ROWS), col),
            device_id_type=pl.DeviceIdType.MESH,
        )
    pl.semaphore_wait(barrier, COLS + ROWS - 2)

    started = []
    row_copies, col_copies = [], []
    for i in range(1, ROWS):
        to = lax.rem(row + i, ROWS)
        copy = push(weighted.at[to], slabs_w.at[row], row_send.at[i], row_recv.at[i], (to, col))
        copy.start()
        row_copies.append(copy)
    for i in range(1, COLS):
        to = lax.rem(col + i, COLS)
        copy = push(plain.at[to], slabs.at[slot], col_send.at[i], col_recv.at[i], (row, to))
        copy.start()
        col_copies.append(copy)
    own_p = pltpu.make_async_copy(plain.at[col], slabs.at[slot], own_sem.at[0])
    own_w = pltpu.make_async_copy(weighted.at[row], slabs_w.at[row], own_sem.at[1])
    own_p.start()
    own_w.start()
    own_w.wait()
    for copy in row_copies:
        copy.wait_recv()
    block = placed(points_w[...], codes_w[...], [slabs_w[i] for i in range(ROWS)], fold_w[...])
    lefts[slot] = jnp.transpose(block, (1, 0)).astype(jnp.bfloat16)
    beside = push(
        lefts.at[slot], lefts.at[slot], left_send.at[0], left_recv.at[0],
        (row, (x * 2 + 1 - y_lo) * 2 + core),
    )
    beside.start()

    own_p.wait()
    for copy in col_copies:
        copy.wait_recv()

    def part(source, tile, half=None):
        if half is None:
            rows = pl.ds(tile * TILE, TILE)
        else:
            rows = pl.ds(tile * TILE + half * (TILE // 2), TILE // 2)
        return panels.at[source].at[rows]

    moves = {}

    def move(tile, kind, source, device, half=None):
        copy = push(
            part(source, tile, half), part(source, tile, half),
            move_send.at[tile * KINDS + kind], move_recv.at[tile * KINDS + kind], device,
        )
        copy.start()
        moves[tile, kind] = copy

    starts, span = windows(G_COL, COLS, TILE)
    for tile in range(TILES):
        window = slice(starts[tile], starts[tile] + span)
        block = placed(
            points_p[tile * TILE : (tile + 1) * TILE], codes_p[:, window],
            [slabs[i, window] for i in range(COLS)], fold_p[...],
        )
        panels[row, tile * TILE : (tile + 1) * TILE, :] = block.astype(jnp.bfloat16)
        move(tile, 0, row, across)
        move(tile, 1, row, above)
        move(tile, 2, row, below)

    first, second = range(3), range(3, TILES)

    def pass_on(tile, y, kinds):
        moves[tile, kinds[0]].wait_recv()
        move(tile, kinds[2], down * 2 + y, (up * 2 + y_hi, col), 0)
        moves[tile, kinds[1]].wait_recv()
        move(tile, kinds[3], up * 2 + y, (down * 2 + y_hi, col), 1)

    for tile in first:
        moves[tile, 0].wait_recv()
        move(tile, 5, across_row, above)
        move(tile, 6, across_row, below)
        pass_on(tile, y_hi, (1, 2, 3, 4))
    beside.wait_recv()
    spread = []
    for i in range(1, 4):
        to = lax.rem(x + i, 4)
        pair = lefts.at[pl.ds(core * 8 + x * 2, 2)]
        copy = push(pair, pair, left_send.at[i], left_recv.at[i], (row, (to * 2 + y_lo) * 2 + core))
        copy.start()
        spread.append(copy)
    for tile in second:
        pass_on(tile, y_hi, (1, 2, 3, 4))
        move(tile, 5, down * 2 + y_hi, across)
        move(tile, 6, up * 2 + y_hi, across)
    for tile in first:
        pass_on(tile, 1 - y_hi, (5, 6, 7, 8))
    for copy in spread:
        copy.wait_recv()
    octet = lefts.at[pl.ds(core * 8, 8)]
    twin = push(octet, octet, left_send.at[4], left_recv.at[4], (row, col + 1 - 2 * core))
    twin.start()
    for tile in second:
        moves[tile, 3].wait_recv()
        move(tile, 7, far * 2 + y_hi, across, 0)
        moves[tile, 4].wait_recv()
        move(tile, 8, far * 2 + y_hi, across, 1)
    twin.wait_recv()
    for source in range(ROWS):
        block = lefts[:, source * 16 : source * 16 + 16, :].reshape(2 * LANES, G_ROW)
        block = jnp.transpose(block.astype(jnp.float32), (1, 0)).astype(jnp.bfloat16)
        lanes = slice(source * 2 * LANES, (source + 1) * 2 * LANES)
        left[:G_ROW, lanes] = block
        left[G_ROW:, lanes] = dot_nn(block, turn[...]).astype(jnp.bfloat16)

    outs = []
    for tile in range(TILES):
        for kind in (3, 4, 7, 8) if tile in first else (0, 5, 6, 7, 8):
            moves[tile, kind].wait_recv()
        total = None
        for source in range(ROWS):
            term = dot_nt(
                left[:, source * 2 * LANES : (source + 1) * 2 * LANES],
                panels[source, tile * TILE : (tile + 1) * TILE, :],
            )
            total = term if total is None else total + term
        if tile >= 2:
            outs[tile - 2].wait()
        stage[tile % 2] = total.reshape(2, G_ROW, TILE)
        copy = pltpu.make_async_copy(
            stage.at[tile % 2], out.at[:, :, pl.ds(tile * TILE, TILE)], out_sem.at[tile % 2]
        )
        copy.start()
        outs.append(copy)
    for copy in row_copies + col_copies + [beside] + spread + [twin]:
        copy.wait_send()
    for copy in moves.values():
        copy.wait_send()
    outs[-2].wait()
    outs[-1].wait()


def exchange(points_p, points_w, codes_p, codes_w, plain, weighted):
    vmem = pl.BlockSpec(memory_space=pltpu.VMEM)
    dma = pltpu.SemaphoreType.DMA
    return pl.pallas_call(
        exchange_kernel,
        in_specs=[vmem] * 9,
        out_specs=pl.BlockSpec(memory_space=pl.ANY),
        out_shape=jax.ShapeDtypeStruct((2, G_ROW, G_COL), jnp.float32),
        scratch_shapes=[
            pltpu.VMEM(plain.shape, jnp.bfloat16),
            pltpu.VMEM(weighted.shape, jnp.bfloat16),
            pltpu.VMEM((COLS, LANES, G_ROW), jnp.bfloat16),
            pltpu.VMEM((2 * G_ROW, ROWS * 2 * LANES), jnp.bfloat16),
            pltpu.VMEM((ROWS, G_COL, 2 * LANES), jnp.bfloat16),
            pltpu.VMEM((2, 2, G_ROW, TILE), jnp.float32),
            dma((COLS,)), dma((COLS,)), dma((ROWS,)), dma((ROWS,)), dma((5,)), dma((5,)),
            dma((TILES * KINDS,)), dma((TILES * KINDS,)), dma((2,)), dma((2,)),
        ],
        compiler_params=pltpu.CompilerParams(
            collective_id=0, has_side_effects=True, vmem_limit_bytes=56 * 2**20
        ),
        name="exchange",
    )(
        points_p, points_w, codes_p, codes_w, plain, weighted,
        jnp.asarray(fold_table(COLS)), jnp.asarray(fold_table(ROWS)), jnp.asarray(turn_table()),
    )


def on_device(val_wave, cond_wave, val_energy, cond_energy, band_owner, grid_map):
    row = lax.axis_index("row")
    col = lax.axis_index("col")
    plain, weighted = spectra(val_wave, cond_wave, val_energy, cond_energy, band_owner)
    codes_p = orbit_lists(G_COL, COLS)[1]
    codes_w = orbit_lists(G_ROW, ROWS)[1]
    points_p = lax.dynamic_slice(grid_map, (col * G_COL,), (G_COL,)).reshape(G_COL, 1)
    points_w = lax.dynamic_slice(grid_map, (row * G_ROW,), (G_ROW,)).reshape(G_ROW, 1)
    return exchange(
        points_p, points_w, jnp.asarray(codes_p)[col], jnp.asarray(codes_w)[row], plain, weighted
    )


def solution(mesh):
    in_specs = (P(), P(("row", "col"), None, None, None), P(), P(), P(("row", "col")), P())
    out_specs = P(None, "row", "col")
    return jax.shard_map(
        on_device, mesh=mesh, in_specs=in_specs, out_specs=out_specs, check_vma=False
    )
```

time: 246 us -> 146 us (0.59)
  waiting for transfers between devices: 115 us -> 0 us
  Pallas kernels: 82.2 us -> 124 us
  starting transfers between devices: 15.1 us -> 0 us
  between operations: 14.2 us -> 0.69 us
    all_gather x2 -> x0, waiting for transfers between devices: 91.6 us -> none  [the longest x1 91.6 us: on_device(): panels = lax.all_gather(panel, 'row', axis=0)]
    pallas_call x3 -> x1, Pallas kernels: 26 us -> 91.2 us  [exchange(): pl.pallas_call(exchange_kernel, in_specs=[vmem] * 9, out_specs=pl.BlockSp...]
    all_to_all x2 -> x0, waiting for transfers between devices: 23.4 us -> none  [the longest x1 17.9 us: on_device(): lax.all_to_all(plain, 'col', split_axis=0, concat_axis=0, tiled=True)]
    pallas_call x1, Pallas kernels: 56.2 us -> 33.3 us  [spectra(): pl.pallas_call(spectrum_kernel, grid=(4,), in_specs=[smem] * 5 + [pl.Bloc...]
    all_to_all x2 -> x0, starting transfers between devices: 15.1 us -> none  [the longest x1 8.5 us: on_device(): lax.all_to_all(weighted, 'row', split_axis=0, concat_axis=0, tiled=True)]
    unnamed x22 -> x21, local copies, waits for them, and re-layouts: 8.79 us -> 12.7 us
  transfers between devices with their start and end apart: 4 -> 0, of which waited for: 3 -> 0; matrix products, arithmetic and copies ran while one was open for 5% -> 0% of each run, Pallas kernels for 6% -> 0%
where the time goes in v1:
time: 146 us; the launch traced here: 144 us
  Pallas kernels  124 us (85%)
  local copies, waits for them, and re-layouts  18.8 us (13%)
    pallas_call x1, Pallas kernels, exchange(): pl.pallas_call(exchange_kernel, in_specs=[vmem] * 9, out_specs=pl.BlockSp...  91.2 us
    pallas_call x1, Pallas kernels, spectra(): pl.pallas_call(spectrum_kernel, grid=(4,), in_specs=[smem] * 5 + [pl.Bloc...  33.3 us
    unnamed x21, local copies, waits for them, and re-layouts  12.7 us

profile of v1, /device:TPU:1, one launch (start us, length us, event | category | flops | bytes accessed | tf_op | source)
XLA Modules:
  0.0 143.9 jit_solution(13757792048398298387)
XLA Ops:
  0.7 1.2 dynamic-slice_bitcast_fusion.1.codes_w
  1.8 0.8 dynamic_slice.13
  2.6 1.3 dynamic-slice_bitcast_fusion.codes_p
  3.9 0.8 dynamic_slice.12
  4.6 0.8 copy.18.points_w
  5.4 1.3 reshape.8.points_p
  6.7 0.0 copy-start.1
  6.7 1.2 copy-done.1
  7.9 0.0 copy-start.2
  7.9 0.9 copy-done.2
  8.8 0.0 copy-start.3
  8.9 0.9 copy-done.3
  9.8 0.0 copy-start.4
  9.8 0.9 copy-done.4
  10.7 0.7 copy-done.6
  11.4 0.7 copy-done.7
  12.1 0.7 copy-done.8
  12.7 0.7 copy-done.9
  13.4 33.3 %spectra.1 = (bf16[16,320,128]{2,1,0:T(8,128)(2,1)S(1)}, bf16[8,64,128]{2,1,0:T(8,128)(2,1)S(1)}) custom-call(s32[1]{0:T(128)S(6)} %copy.20.owner, f32[128]{0:T(128)S(1)} %copy-done.8, f32[8]{0:T(128)S(1)} %copy-done.9, s32[5120]{0:T(1024)S(1)} %copy-done.6, s32[512]{0:T(512)S(1)} %copy-done.7, bf16[8,64,64,128]{3,2,1,0:T(8,128)(2,1)} %val.1, ...), custom_call_target="tpu_custom_call" | custom-call | tf_op jit(solution)/shard_map/spectra/pallas_call | solution.py:239
  46.7 0.0 copy-start
  46.7 1.0 copy-done
  47.7 0.7 copy-done.5
  48.4 91.2 %exchange.1 = f32[2,256,1920]{2,1,0:T(8,128)} custom-call(s32[1920,1]{1,0:T(8,128)} %reshape.8.points_p, s32[256,1]{1,0:T(8,128)} %copy.18.points_w, s32[1,320]{1,0:T(1,128)} %dynamic-slice_bitcast_fusion.codes_p, s32[1,64]{1,0:T(1,128)} %dynamic-slice_bitcast_fusion.1.codes_w, bf16[16,320,128]{2,1,0:T(8,128)(2,1)} %copy-done, ...), custom_call_target="tpu_custom_call" | custom-call | tf_op jit(solution)/shard_map/exchange/pallas_call | solution.py:482
  139.6 4.3 %copy.21 = f32[2,256,1920]{2,1,0:T(8,128)} copy(f32[2,256,1920]{2,1,0:T(8,128)} %exchange.1) | data formatting | bytes 7864320
  (5 shorter events, 0.0 us)
Async XLA Ops:
  6.7 1.2 copy-start.1
  7.9 0.9 copy-start.2
  8.8 0.9 copy-start.3
  9.8 0.9 copy-start.4
  10.7 0.7 copy-start.6
  11.4 0.7 copy-start.7
  12.1 0.7 copy-start.8
  12.7 0.7 copy-start.9
  46.7 1.1 copy-start
  47.7 0.7 copy-start.5
